TPU v7x, 32 devices: a whole 2x2x4 slice. The times are simulated.
32 devices in a mesh: row: 16 (over z, y, x), rep: 2 (over core).
Axes of the slice: x: 2, y: 2, z: 4, core: 2. Of those that a mesh axis runs over, the one named last changes fastest.
Arguments:
- features: bfloat16 [8192, 256], P('row'), may hold values from -6 to 6
- weight: bfloat16 [256, 256], replicated, may hold values from -0.375 to 0.375
- bias: float32 [256], replicated, may hold values from -3 to 3
- cotangent: bfloat16 [8192, 256], P(('row', 'rep')), may hold values from -14 to 14
- tile_values: bfloat16 [16, 16, 8, 128, 128], P('row', 'rep'), may hold values from -0.125 to 0.125
- tile_index: int32 [16, 16, 8, 2], P('row', 'rep'), may hold values from 0 to 3
- tile_count: int32 [16, 16], P('row', 'rep'), may hold values from 0 to 8, as said below
- rev_values: bfloat16 [16, 16, 8, 128, 128], P('row', 'rep'), may hold values from -0.125 to 0.125
- rev_index: int32 [16, 16, 8, 2], P('row', 'rep'), may hold values from 0 to 3
- rev_count: int32 [16, 16], P('row', 'rep'), may hold values from 0 to 8, as said below
Outputs:
- activations: bfloat16 [8192, 256], P(('row', 'rep'))
- grad_features: bfloat16 [8192, 256], P(('row', 'rep'))
- grad_weight: float32 [256, 256], replicated
- grad_bias: float32 [256], replicated
Inputs may be any that keep to these rules, and one draw needn't show every extreme that they name: Slots t < tile_count[a, d] are used; some slab pair uses all 8 slots in every draw. Slots t < rev_count[a, d] are used; some slab pair uses all 8 slots in every draw.
All inputs are finite; a program needn't handle non-finite values.
Results may differ from a plain program's by a relative error of at most 0.006.
Values may be sent and summed in bfloat16 or wider, within the bound.
A program may use at most 64 MiB of HBM per device.

v0:
```python
import jax
import jax.numpy as jnp
from jax import lax
from jax.sharding import PartitionSpec as P

TILE = 128
BLOCKS = 4


def passed_along(value, axis, steps):
    count = lax.axis_size(axis)
    pairs = [(source, (source + steps) % count) for source in range(count)]
    return lax.ppermute(value, axis, pairs)


def section_term(current, tile_block, slot_index, counts):
    blocks = current.reshape(BLOCKS, TILE, current.shape[1])
    sources = jnp.take(blocks, slot_index[:, 1], axis=0)
    product = jnp.einsum("tab,tbf->taf", tile_block, sources, preferred_element_type=jnp.float32)
    usable = jnp.arange(slot_index.shape[0], dtype=jnp.int32) < counts
    placing = (
        (slot_index[:, 0][None, :] == jnp.arange(BLOCKS, dtype=jnp.int32)[:, None])
        & usable[None, :]
    ).astype(jnp.float32)
    return jnp.einsum("nt,taf->naf", placing, product, precision=lax.Precision.HIGHEST)


def first_source(source, sections):
    rep_index = lax.axis_index("rep")
    groups = lax.axis_size("rep")
    current = source
    for shift_bit in range(groups.bit_length() - 1):
        shifted = passed_along(current, "row", -(sections << shift_bit))
        current = jnp.where(rep_index >> shift_bit & 1 == 1, shifted, current)
    return current


def apply_tiles(source, values, slot_index, counts):
    sections = values.shape[1]
    current = first_source(source, sections)
    summed_rows = jnp.zeros((BLOCKS, TILE, source.shape[1]), jnp.float32)
    for section in range(sections):
        if section > 0:
            current = passed_along(current, "row", -1)
        summed_rows = summed_rows + section_term(
            current, values[0, section], slot_index[0, section], counts[0, section]
        )
    return summed_rows.reshape(source.shape[0], source.shape[1])


def reduce_part(partial_rows):
    return lax.psum(partial_rows, "rep")


def own_rows(matrix):
    share_size = matrix.shape[0] // lax.axis_size("rep")
    return lax.dynamic_slice_in_dim(matrix, lax.axis_index("rep") * share_size, share_size, 0)


def activate(preact, cotangent):
    sigmoid_pre = jax.nn.sigmoid(preact)
    activations = (preact * sigmoid_pre).astype(jnp.bfloat16)
    grad_pre = (
        cotangent.astype(jnp.float32) * sigmoid_pre * (1.0 + preact * (1.0 - sigmoid_pre))
    ).astype(jnp.bfloat16)
    return (activations, grad_pre)


def local(
    features,
    weight,
    bias,
    cotangent,
    tile_values,
    tile_index,
    tile_count,
    rev_values,
    rev_index,
    rev_count,
):
    node_total = features.shape[0] * lax.axis_size("row")
    grad_scale = float(node_total) ** (-0.5)
    summed = reduce_part(apply_tiles(features, tile_values, tile_index, tile_count))
    mixed_all = summed.astype(jnp.bfloat16)
    preact_all = jnp.dot(mixed_all, weight, preferred_element_type=jnp.float32) + bias
    cotangent_all = lax.all_gather(cotangent, "rep", axis=0, tiled=True)
    activ_all, grad_all = activate(preact_all, cotangent_all)
    image = jnp.einsum("ng,fg->nf", grad_all, weight, preferred_element_type=jnp.float32).astype(
        jnp.bfloat16
    )
    mixed_rows = own_rows(mixed_all)
    grad_pre = own_rows(grad_all)
    activations = own_rows(activ_all)
    weight_term = jnp.einsum("nf,ng->fg", mixed_rows, grad_pre, preferred_element_type=jnp.float32)
    bias_term = jnp.sum(grad_pre.astype(jnp.float32), axis=0)
    grad_weight, grad_bias = lax.psum((weight_term, bias_term), ("row", "rep"))
    back_rows = reduce_part(apply_tiles(image, rev_values, rev_index, rev_count))
    back_rows = own_rows(back_rows)
    return (
        activations,
        back_rows.astype(jnp.bfloat16),
        grad_weight * grad_scale,
        grad_bias * grad_scale,
    )


def solution(mesh):
    placed = (
        P("row", None),
        P(),
        P(),
        P(("row", "rep"), None),
        P("row", "rep", None, None, None),
        P("row", "rep", None, None),
        P("row", "rep"),
        P("row", "rep", None, None, None),
        P("row", "rep", None, None),
        P("row", "rep"),
    )
    return jax.shard_map(
        local,
        mesh=mesh,
        in_specs=placed,
        out_specs=(P(("row", "rep"), None), P(("row", "rep"), None), P(), P()),
        check_vma=False,
    )
```

profile of v0, /device:TPU:0, one launch (start us, length us, event | category | flops | bytes accessed | tf_op | source)
XLA Modules:
  0.0 381.1 jit_solution(8210804947538525664)
XLA Ops:
  7.2 4.1 %collective-permute-start = (bf16[512,256]{1,0:T(8,128)(2,1)}, bf16[512,256]{1,0:T(8,128)(2,1)S(1)}, u32[]{:S(2)}, u32[]{:S(2)}) collective-permute-start(bf16[512,256]{1,0:T(8,128)(2,1)} %param.12), channel_id=1, source_target_pairs={{0,16},{2,18},{4,20},{6,22},{8,24},{10,26},{12,28},{14,30},{16,0},... | collective-permute-start | bytes 786440 | tf_op jit(solution)/shard_map/ppermute | solution.py:13
  23.6 1.6 fusion.216
  25.8 1.2 iota_compare_fusion.30
  38.3 1.6 fusion.215
  49.1 1.3 iota_compare_fusion.17
  52.1 3.5 all_gather.3
  57.3 3.3 collective-permute-start.1
  61.1 1.4 fusion.48
  63.6 2.1 collective-permute-done.1
  66.3 1.4 fusion.46
  68.1 6.1 %collective-permute-start.2 = (bf16[512,256]{1,0:T(8,128)(2,1)S(1)}, bf16[512,256]{1,0:T(8,128)(2,1)S(1)}, u32[]{:S(2)}, u32[]{:S(2)}) collective-permute-start(bf16[512,256]{1,0:T(8,128)(2,1)S(1)} %collective-permute-done.1), channel_id=1, source_target_pairs={{0,30},{2,0},{4,2},{6,4},{8,6},{10,8},{12,10},{14,12},{16,14},{18,... | collective-permute-start | bytes 786440 | tf_op jit(solution)/shard_map/ppermute | solution.py:13
  74.3 1.3 convolution_add_fusion.13
  75.6 2.9 collective-permute-done.2
  79.2 1.4 fusion.44
  81.1 6.1 %collective-permute-start.3 = (bf16[512,256]{1,0:T(8,128)(2,1)S(1)}, bf16[512,256]{1,0:T(8,128)(2,1)S(1)}, u32[]{:S(2)}, u32[]{:S(2)}) collective-permute-start(bf16[512,256]{1,0:T(8,128)(2,1)S(1)} %copy-done.2), channel_id=1, source_target_pairs={{0,30},{2,0},{4,2},{6,4},{8,6},{10,8},{12,10},{14,12},{16,14},{18,... | collective-permute-start | bytes 786440 | tf_op jit(solution)/shard_map/ppermute | solution.py:13
  87.3 1.3 convolution_add_fusion.12
  88.5 2.6 collective-permute-done.3
  91.9 1.4 fusion.42
  93.8 6.1 %collective-permute-start.4 = (bf16[512,256]{1,0:T(8,128)(2,1)S(1)}, bf16[512,256]{1,0:T(8,128)(2,1)S(1)}, u32[]{:S(2)}, u32[]{:S(2)}) collective-permute-start(bf16[512,256]{1,0:T(8,128)(2,1)S(1)} %copy-done.4), channel_id=1, source_target_pairs={{0,30},{2,0},{4,2},{6,4},{8,6},{10,8},{12,10},{14,12},{16,14},{18,... | collective-permute-start | bytes 786440 | tf_op jit(solution)/shard_map/ppermute | solution.py:13
  99.9 1.3 convolution_add_fusion.11
  101.2 2.6 collective-permute-done.4
  104.6 1.4 fusion.40
  106.5 6.1 %collective-permute-start.5 = (bf16[512,256]{1,0:T(8,128)(2,1)S(1)}, bf16[512,256]{1,0:T(8,128)(2,1)S(1)}, u32[]{:S(2)}, u32[]{:S(2)}) collective-permute-start(bf16[512,256]{1,0:T(8,128)(2,1)S(1)} %copy-done.6), channel_id=1, source_target_pairs={{0,30},{2,0},{4,2},{6,4},{8,6},{10,8},{12,10},{14,12},{16,14},{18,... | collective-permute-start | bytes 786440 | tf_op jit(solution)/shard_map/ppermute | solution.py:13
  112.6 1.3 convolution_add_fusion.10
  113.9 2.6 collective-permute-done.5
  117.2 1.4 fusion.38
  119.1 6.1 %collective-permute-start.6 = (bf16[512,256]{1,0:T(8,128)(2,1)S(1)}, bf16[512,256]{1,0:T(8,128)(2,1)S(1)}, u32[]{:S(2)}, u32[]{:S(2)}) collective-permute-start(bf16[512,256]{1,0:T(8,128)(2,1)S(1)} %copy-done.8), channel_id=1, source_target_pairs={{0,30},{2,0},{4,2},{6,4},{8,6},{10,8},{12,10},{14,12},{16,14},{18,... | collective-permute-start | bytes 786440 | tf_op jit(solution)/shard_map/ppermute | solution.py:13
  125.3 1.3 convolution_add_fusion.9
  126.6 2.6 collective-permute-done.6
  129.9 1.4 fusion.36
  131.8 6.3 %collective-permute-start.7 = (bf16[512,256]{1,0:T(8,128)(2,1)S(1)}, bf16[512,256]{1,0:T(8,128)(2,1)S(1)}, u32[]{:S(2)}, u32[]{:S(2)}) collective-permute-start(bf16[512,256]{1,0:T(8,128)(2,1)S(1)} %copy-done.10), channel_id=1, source_target_pairs={{0,30},{2,0},{4,2},{6,4},{8,6},{10,8},{12,10},{14,12},{16,14},{18,... | collective-permute-start | bytes 786440 | tf_op jit(solution)/shard_map/ppermute | solution.py:13
  138.1 1.3 convolution_add_fusion.8
  139.4 2.6 collective-permute-done.7
  142.7 1.4 fusion.34
  145.4 4.8 %all-reduce.5 = bf16[512,256]{1,0:T(8,128)(2,1)S(1)} all-reduce(f32[512,256]{1,0:T(8,128)S(1)} %bitcast.296), channel_id=1, replica_groups=mesh['row'=16,'rep'=2] {'rep'}, use_global_device_ids=true, to_apply=%region_0.2 | all-reduce | flops 131072 | bytes 786432 | tf_op jit(solution)/shard_map/psum | solution.py:52
  152.0 43.5 %psum.31 = f32[256]{0:T(256)S(1)} all-reduce(f32[256]{0:T(256)S(1)} %convert_reduce_fusion), channel_id=1, replica_groups=mesh['row'=16,'rep'=2] {'row','rep'}, use_global_device_ids=true, to_apply=%region_4.6 | all-reduce | flops 256 | bytes 2048 | tf_op jit(solution)/shard_map/psum | solution.py:96
  196.7 82.9 %all-reduce.4.cloned.1.call-done = f32[256,256]{1,0:T(8,128)} async-done(((f32[256,256]{1,0:T(8,128)}), f32[256,256]{1,0:T(8,128)}) %all-reduce.4.cloned.1.call-update) | async-done | bytes 262160 | tf_op jit(solution)/shard_map/psum | solution.py:96
  279.6 1.7 broadcast_multiply_fusion
  281.3 3.3 collective-permute-start.9
  285.4 1.4 fusion.32
  287.9 1.5 collective-permute-done.9
  290.1 1.4 fusion.30
  292.0 6.1 %collective-permute-start.10 = (bf16[512,256]{1,0:T(8,128)(2,1)S(1)}, bf16[512,256]{1,0:T(8,128)(2,1)S(1)}, u32[]{:S(2)}, u32[]{:S(2)}) collective-permute-start(bf16[512,256]{1,0:T(8,128)(2,1)S(1)} %collective-permute-done.9), channel_id=1, source_target_pairs={{0,30},{2,0},{4,2},{6,4},{8,6},{10,8},{12,10},{14,12},{16,14},{18,... | collective-permute-start | bytes 786440 | tf_op jit(solution)/shard_map/ppermute | solution.py:13
  298.1 1.3 convolution_add_fusion.6
  299.4 2.6 collective-permute-done.10
  302.7 1.4 fusion.28
  304.7 6.1 %collective-permute-start.11 = (bf16[512,256]{1,0:T(8,128)(2,1)S(1)}, bf16[512,256]{1,0:T(8,128)(2,1)S(1)}, u32[]{:S(2)}, u32[]{:S(2)}) collective-permute-start(bf16[512,256]{1,0:T(8,128)(2,1)S(1)} %copy-done.12), channel_id=1, source_target_pairs={{0,30},{2,0},{4,2},{6,4},{8,6},{10,8},{12,10},{14,12},{16,14},{18,... | collective-permute-start | bytes 786440 | tf_op jit(solution)/shard_map/ppermute | solution.py:13
  310.8 1.3 convolution_add_fusion.5
  312.1 2.6 collective-permute-done.11
  315.4 1.4 fusion.26
  317.3 6.1 %collective-permute-start.12 = (bf16[512,256]{1,0:T(8,128)(2,1)S(1)}, bf16[512,256]{1,0:T(8,128)(2,1)S(1)}, u32[]{:S(2)}, u32[]{:S(2)}) collective-permute-start(bf16[512,256]{1,0:T(8,128)(2,1)S(1)} %copy-done.14), channel_id=1, source_target_pairs={{0,30},{2,0},{4,2},{6,4},{8,6},{10,8},{12,10},{14,12},{16,14},{18,... | collective-permute-start | bytes 786440 | tf_op jit(solution)/shard_map/ppermute | solution.py:13
  323.5 1.3 convolution_add_fusion.4
  324.7 2.6 collective-permute-done.12
  328.1 1.4 fusion.24
  330.0 6.4 %collective-permute-start.13 = (bf16[512,256]{1,0:T(8,128)(2,1)S(1)}, bf16[512,256]{1,0:T(8,128)(2,1)S(1)}, u32[]{:S(2)}, u32[]{:S(2)}) collective-permute-start(bf16[512,256]{1,0:T(8,128)(2,1)S(1)} %copy-done.16), channel_id=1, source_target_pairs={{0,30},{2,0},{4,2},{6,4},{8,6},{10,8},{12,10},{14,12},{16,14},{18,... | collective-permute-start | bytes 786440 | tf_op jit(solution)/shard_map/ppermute | solution.py:13
  337.5 2.7 collective-permute-done.13
  340.9 1.4 fusion.22
  342.8 6.1 %collective-permute-start.14 = (bf16[512,256]{1,0:T(8,128)(2,1)S(1)}, bf16[512,256]{1,0:T(8,128)(2,1)S(1)}, u32[]{:S(2)}, u32[]{:S(2)}) collective-permute-start(bf16[512,256]{1,0:T(8,128)(2,1)S(1)} %copy-done.18), channel_id=1, source_target_pairs={{0,30},{2,0},{4,2},{6,4},{8,6},{10,8},{12,10},{14,12},{16,14},{18,... | collective-permute-start | bytes 786440 | tf_op jit(solution)/shard_map/ppermute | solution.py:13
  349.6 3.3 collective-permute-done.14
  353.6 1.4 fusion.20
  355.5 6.1 %collective-permute-start.15 = (bf16[512,256]{1,0:T(8,128)(2,1)S(1)}, bf16[512,256]{1,0:T(8,128)(2,1)S(1)}, u32[]{:S(2)}, u32[]{:S(2)}) collective-permute-start(bf16[512,256]{1,0:T(8,128)(2,1)S(1)} %copy-done.20), channel_id=1, source_target_pairs={{0,30},{2,0},{4,2},{6,4},{8,6},{10,8},{12,10},{14,12},{16,14},{18,... | collective-permute-start | bytes 786440 | tf_op jit(solution)/shard_map/ppermute | solution.py:13
  362.3 3.3 collective-permute-done.15
  366.1 1.4 fusion.18
  368.7 4.8 %all-reduce.6 = bf16[512,256]{1,0:T(8,128)(2,1)S(1)} all-reduce(f32[512,256]{1,0:T(8,128)S(1)} %bitcast.297), channel_id=1, replica_groups=mesh['row'=16,'rep'=2] {'rep'}, use_global_device_ids=true, to_apply=%region_1.3 | all-reduce | flops 131072 | bytes 786432 | tf_op jit(solution)/shard_map/psum | solution.py:52
  (185 shorter events, 63.9 us)
Async XLA Ops:
  7.2 143.1 %copy-start = (bf16[256,256]{1,0:T(8,128)(2,1)S(1)}, bf16[256,256]{1,0:T(8,128)(2,1)}, u32[]{:S(2)}) copy-start(bf16[256,256]{1,0:T(8,128)(2,1)} %param.13) | copy-start | bytes 393220
  7.2 272.4 %all-reduce.4.cloned.1.call-start = ((), (), s32[]{:S(2)}) async-start(), calls=%async_computation | async-start | bytes 524288 | tf_op jit(solution)/shard_map/psum | solution.py:96
  7.2 49.0 %collective-permute-start = (bf16[512,256]{1,0:T(8,128)(2,1)}, bf16[512,256]{1,0:T(8,128)(2,1)S(1)}, u32[]{:S(2)}, u32[]{:S(2)}) collective-permute-start(bf16[512,256]{1,0:T(8,128)(2,1)} %param.12), channel_id=1, source_target_pairs={{0,16},{2,18},{4,20},{6,22},{8,24},{10,26},{12,28},{14,30},{16,0},... | collective-permute-start | bytes 786440 | tf_op jit(solution)/shard_map/ppermute | solution.py:13
  57.3 8.4 %collective-permute-start.1 = (bf16[512,256]{1,0:T(8,128)(2,1)S(1)}, bf16[512,256]{1,0:T(8,128)(2,1)S(1)}, u32[]{:S(2)}, u32[]{:S(2)}) collective-permute-start(bf16[512,256]{1,0:T(8,128)(2,1)S(1)} %broadcast_select_fusion.1), channel_id=1, source_target_pairs={{0,30},{2,0},{4,2},{6,4},{8,6},{10,8},{12,10},{14,12},{16,14},{18,... | collective-permute-start | bytes 786440 | tf_op jit(solution)/shard_map/ppermute | solution.py:13
  68.1 10.4 %collective-permute-start.2 = (bf16[512,256]{1,0:T(8,128)(2,1)S(1)}, bf16[512,256]{1,0:T(8,128)(2,1)S(1)}, u32[]{:S(2)}, u32[]{:S(2)}) collective-permute-start(bf16[512,256]{1,0:T(8,128)(2,1)S(1)} %collective-permute-done.1), channel_id=1, source_target_pairs={{0,30},{2,0},{4,2},{6,4},{8,6},{10,8},{12,10},{14,12},{16,14},{18,... | collective-permute-start | bytes 786440 | tf_op jit(solution)/shard_map/ppermute | solution.py:13
  78.5 0.7 copy-start.1
  79.2 1.9 copy-start.2
  81.1 10.0 %collective-permute-start.3 = (bf16[512,256]{1,0:T(8,128)(2,1)S(1)}, bf16[512,256]{1,0:T(8,128)(2,1)S(1)}, u32[]{:S(2)}, u32[]{:S(2)}) collective-permute-start(bf16[512,256]{1,0:T(8,128)(2,1)S(1)} %copy-done.2), channel_id=1, source_target_pairs={{0,30},{2,0},{4,2},{6,4},{8,6},{10,8},{12,10},{14,12},{16,14},{18,... | collective-permute-start | bytes 786440 | tf_op jit(solution)/shard_map/ppermute | solution.py:13
  91.2 0.7 copy-start.3
  91.9 1.9 copy-start.4
  93.8 10.0 %collective-permute-start.4 = (bf16[512,256]{1,0:T(8,128)(2,1)S(1)}, bf16[512,256]{1,0:T(8,128)(2,1)S(1)}, u32[]{:S(2)}, u32[]{:S(2)}) collective-permute-start(bf16[512,256]{1,0:T(8,128)(2,1)S(1)} %copy-done.4), channel_id=1, source_target_pairs={{0,30},{2,0},{4,2},{6,4},{8,6},{10,8},{12,10},{14,12},{16,14},{18,... | collective-permute-start | bytes 786440 | tf_op jit(solution)/shard_map/ppermute | solution.py:13
  103.8 0.7 copy-start.5
  104.5 1.9 copy-start.6
  106.5 10.0 %collective-permute-start.5 = (bf16[512,256]{1,0:T(8,128)(2,1)S(1)}, bf16[512,256]{1,0:T(8,128)(2,1)S(1)}, u32[]{:S(2)}, u32[]{:S(2)}) collective-permute-start(bf16[512,256]{1,0:T(8,128)(2,1)S(1)} %copy-done.6), channel_id=1, source_target_pairs={{0,30},{2,0},{4,2},{6,4},{8,6},{10,8},{12,10},{14,12},{16,14},{18,... | collective-permute-start | bytes 786440 | tf_op jit(solution)/shard_map/ppermute | solution.py:13
  116.5 0.7 copy-start.7
  117.2 1.9 copy-start.8
  119.1 10.0 %collective-permute-start.6 = (bf16[512,256]{1,0:T(8,128)(2,1)S(1)}, bf16[512,256]{1,0:T(8,128)(2,1)S(1)}, u32[]{:S(2)}, u32[]{:S(2)}) collective-permute-start(bf16[512,256]{1,0:T(8,128)(2,1)S(1)} %copy-done.8), channel_id=1, source_target_pairs={{0,30},{2,0},{4,2},{6,4},{8,6},{10,8},{12,10},{14,12},{16,14},{18,... | collective-permute-start | bytes 786440 | tf_op jit(solution)/shard_map/ppermute | solution.py:13
  129.2 0.7 copy-start.9
  129.9 1.9 copy-start.10
  131.8 10.2 %collective-permute-start.7 = (bf16[512,256]{1,0:T(8,128)(2,1)S(1)}, bf16[512,256]{1,0:T(8,128)(2,1)S(1)}, u32[]{:S(2)}, u32[]{:S(2)}) collective-permute-start(bf16[512,256]{1,0:T(8,128)(2,1)S(1)} %copy-done.10), channel_id=1, source_target_pairs={{0,30},{2,0},{4,2},{6,4},{8,6},{10,8},{12,10},{14,12},{16,14},{18,... | collective-permute-start | bytes 786440 | tf_op jit(solution)/shard_map/ppermute | solution.py:13
  142.7 1.9 copy-start.27
  142.7 1.9 copy-start.35
  144.6 5.6 %copy-start.21 = (bf16[512,256]{1,0:T(8,128)(2,1)S(1)}, bf16[512,256]{1,0:T(8,128)(2,1)}, u32[]{:S(2)}) copy-start(bf16[512,256]{1,0:T(8,128)(2,1)} %all_gather.3) | copy-start | bytes 786436
  144.6 5.6 %copy-start.36 = (f32[256]{0:T(256)S(1)}, f32[256]{0:T(256)}, u32[]{:S(2)}) copy-start(f32[256]{0:T(256)} %param.14) | copy-start | bytes 3076
  150.9 134.5 %copy-start.33 = (pred[8]{0:T(512)(128)(4,1)S(1)}, pred[8]{0:T(512)(128)(4,1)}, u32[]{:S(2)}) copy-start(pred[8]{0:T(512)(128)(4,1)} %get-tuple-element.19) | copy-start | bytes 28
  151.9 129.4 %collective-permute-start.8 = (bf16[512,256]{1,0:T(8,128)(2,1)S(1)}, bf16[512,256]{1,0:T(8,128)(2,1)S(1)}, u32[]{:S(2)}, u32[]{:S(2)}) collective-permute-start(bf16[512,256]{1,0:T(8,128)(2,1)S(1)} %convolution_convert_fusion), channel_id=1, source_target_pairs={{0,16},{2,18},{4,20},{6,22},{8,24},{10,26},{12,28},{14,30},{16,0},... | collective-permute-start | bytes 786440 | tf_op jit(solution)/shard_map/ppermute | solution.py:13
  281.3 8.1 %collective-permute-start.9 = (bf16[512,256]{1,0:T(8,128)(2,1)S(1)}, bf16[512,256]{1,0:T(8,128)(2,1)S(1)}, u32[]{:S(2)}, u32[]{:S(2)}) collective-permute-start(bf16[512,256]{1,0:T(8,128)(2,1)S(1)} %broadcast_select_fusion), channel_id=1, source_target_pairs={{0,30},{2,0},{4,2},{6,4},{8,6},{10,8},{12,10},{14,12},{16,14},{18,... | collective-permute-start | bytes 786440 | tf_op jit(solution)/shard_map/ppermute | solution.py:13
  285.3 1.9 copy-start.22
  285.3 1.9 copy-start.28
  286.7 3.4 copy-start.31
  292.0 10.0 %collective-permute-start.10 = (bf16[512,256]{1,0:T(8,128)(2,1)S(1)}, bf16[512,256]{1,0:T(8,128)(2,1)S(1)}, u32[]{:S(2)}, u32[]{:S(2)}) collective-permute-start(bf16[512,256]{1,0:T(8,128)(2,1)S(1)} %collective-permute-done.9), channel_id=1, source_target_pairs={{0,30},{2,0},{4,2},{6,4},{8,6},{10,8},{12,10},{14,12},{16,14},{18,... | collective-permute-start | bytes 786440 | tf_op jit(solution)/shard_map/ppermute | solution.py:13
  302.0 0.7 copy-start.11
  302.7 1.9 copy-start.12
  304.7 10.0 %collective-permute-start.11 = (bf16[512,256]{1,0:T(8,128)(2,1)S(1)}, bf16[512,256]{1,0:T(8,128)(2,1)S(1)}, u32[]{:S(2)}, u32[]{:S(2)}) collective-permute-start(bf16[512,256]{1,0:T(8,128)(2,1)S(1)} %copy-done.12), channel_id=1, source_target_pairs={{0,30},{2,0},{4,2},{6,4},{8,6},{10,8},{12,10},{14,12},{16,14},{18,... | collective-permute-start | bytes 786440 | tf_op jit(solution)/shard_map/ppermute | solution.py:13
  314.7 0.7 copy-start.13
  315.4 1.9 copy-start.14
  317.3 10.0 %collective-permute-start.12 = (bf16[512,256]{1,0:T(8,128)(2,1)S(1)}, bf16[512,256]{1,0:T(8,128)(2,1)S(1)}, u32[]{:S(2)}, u32[]{:S(2)}) collective-permute-start(bf16[512,256]{1,0:T(8,128)(2,1)S(1)} %copy-done.14), channel_id=1, source_target_pairs={{0,30},{2,0},{4,2},{6,4},{8,6},{10,8},{12,10},{14,12},{16,14},{18,... | collective-permute-start | bytes 786440 | tf_op jit(solution)/shard_map/ppermute | solution.py:13
  327.3 0.7 copy-start.15
  328.1 8.3 %copy-start.24 = (s32[8]{0:T(128)S(1)}, s32[8]{0:T(128)}, u32[]{:S(2)}) copy-start(s32[8]{0:T(128)} %get-tuple-element.83) | copy-start | bytes 100
  328.1 1.9 copy-start.16
  330.0 10.2 %collective-permute-start.13 = (bf16[512,256]{1,0:T(8,128)(2,1)S(1)}, bf16[512,256]{1,0:T(8,128)(2,1)S(1)}, u32[]{:S(2)}, u32[]{:S(2)}) collective-permute-start(bf16[512,256]{1,0:T(8,128)(2,1)S(1)} %copy-done.16), channel_id=1, source_target_pairs={{0,30},{2,0},{4,2},{6,4},{8,6},{10,8},{12,10},{14,12},{16,14},{18,... | collective-permute-start | bytes 786440 | tf_op jit(solution)/shard_map/ppermute | solution.py:13
  340.2 0.7 copy-start.17
  340.9 8.1 %copy-start.23 = (s32[8]{0:T(128)S(1)}, s32[8]{0:T(128)}, u32[]{:S(2)}) copy-start(s32[8]{0:T(128)} %get-tuple-element.82) | copy-start | bytes 100
  340.9 8.1 %copy-start.34 = (pred[8]{0:T(512)(128)(4,1)S(1)}, pred[8]{0:T(512)(128)(4,1)}, u32[]{:S(2)}) copy-start(pred[8]{0:T(512)(128)(4,1)} %iota_compare_fusion.18) | copy-start | bytes 28
  340.9 1.9 copy-start.18
  342.8 10.0 %collective-permute-start.14 = (bf16[512,256]{1,0:T(8,128)(2,1)S(1)}, bf16[512,256]{1,0:T(8,128)(2,1)S(1)}, u32[]{:S(2)}, u32[]{:S(2)}) collective-permute-start(bf16[512,256]{1,0:T(8,128)(2,1)S(1)} %copy-done.18), channel_id=1, source_target_pairs={{0,30},{2,0},{4,2},{6,4},{8,6},{10,8},{12,10},{14,12},{16,14},{18,... | collective-permute-start | bytes 786440 | tf_op jit(solution)/shard_map/ppermute | solution.py:13
  352.9 0.7 copy-start.19
  353.6 8.1 %copy-start.26 = (s32[8]{0:T(128)S(1)}, s32[8]{0:T(128)}, u32[]{:S(2)}) copy-start(s32[8]{0:T(128)} %get-tuple-element.81) | copy-start | bytes 100
  353.6 8.1 %copy-start.32 = (pred[8]{0:T(512)(128)(4,1)S(1)}, pred[8]{0:T(512)(128)(4,1)}, u32[]{:S(2)}) copy-start(pred[8]{0:T(512)(128)(4,1)} %iota_compare_fusion.17) | copy-start | bytes 28
  353.6 1.9 copy-start.20
  355.5 10.6 %copy-start.30 = (pred[8]{0:T(512)(128)(4,1)S(1)}, pred[8]{0:T(512)(128)(4,1)}, u32[]{:S(2)}) copy-start(pred[8]{0:T(512)(128)(4,1)} %get-tuple-element.5) | copy-start | bytes 28
  355.5 10.0 %collective-permute-start.15 = (bf16[512,256]{1,0:T(8,128)(2,1)S(1)}, bf16[512,256]{1,0:T(8,128)(2,1)S(1)}, u32[]{:S(2)}, u32[]{:S(2)}) collective-permute-start(bf16[512,256]{1,0:T(8,128)(2,1)S(1)} %copy-done.20), channel_id=1, source_target_pairs={{0,30},{2,0},{4,2},{6,4},{8,6},{10,8},{12,10},{14,12},{16,14},{18,... | collective-permute-start | bytes 786440 | tf_op jit(solution)/shard_map/ppermute | solution.py:13
  366.1 1.9 copy-start.25
  366.1 1.9 copy-start.29
Sparse Core Ops, SparseCore 0:
  152.1 127.4 all-reduce.3
where the time goes:
time: 382 us; the launch traced here: 381 us
  waiting for transfers between devices  119 us (31%)
  starting transfers between devices  84.8 us (22%)
  blocking collectives  56.7 us (15%)
  matrix products  40.4 us (11%)
  other arithmetic  35.9 us (9%)
  local copies, waits for them, and re-layouts  28.9 us (8%)
  between operations  15 us (4%)
    ppermute x16, starting transfers between devices, passed_along(): return lax.ppermute(value, axis, pairs)  84.7 us
    psum x1, waiting for transfers between devices, local(): grad_weight, grad_bias = lax.psum((weight_term, bias_term), ('row', 'rep'))  82.9 us
    psum x1, blocking collectives, local(): grad_weight, grad_bias = lax.psum((weight_term, bias_term), ('row', 'rep'))  43.5 us
    ppermute x16, waiting for transfers between devices, passed_along(): return lax.ppermute(value, axis, pairs)  36.6 us
    dot_general x16, matrix products, section_term(): jnp.einsum('tab,tbf->taf', tile_block, sources, preferred_element_type=jn...  22.4 us
    lt x16, other arithmetic, section_term(): usable = jnp.arange(slot_index.shape[0], dtype=jnp.int32) < counts  18.2 us
    dot_general x16, matrix products, section_term(): jnp.einsum('nt,taf->naf', placing, product, precision=lax.Precision.HIGHEST)  16.4 us
    gather x16, local copies, waits for them, and re-layouts, section_term(): sources = jnp.take(blocks, slot_index[:, 1], axis=0)  10.5 us
  transfers between devices with their start and end apart: 17, of which 15 were waited for; matrix products, arithmetic and copies ran while one was open for 17% of the time, Pallas kernels for 0%

commit v1 on v0

--- a/solution.py
+++ b/solution.py
@@ -93,7 +93,7 @@
     activations = own_rows(activ_all)
     weight_term = jnp.einsum("nf,ng->fg", mixed_rows, grad_pre, preferred_element_type=jnp.float32)
     bias_term = jnp.sum(grad_pre.astype(jnp.float32), axis=0)
-    grad_weight, grad_bias = lax.psum((weight_term, bias_term), ("row", "rep"))
+    grad_weight, grad_bias = lax.psum(lax.psum((weight_term, bias_term), "rep"), "row")
     back_rows = reduce_part(apply_tiles(image, rev_values, rev_index, rev_count))
     back_rows = own_rows(back_rows)
     return (

time: 382 us -> 422 us (1.10)
  waiting for transfers between devices: 119 us -> 159 us
    psum x1 -> x2, waiting for transfers between devices: 82.9 us -> 118 us  [the longest x1 113 us: local(): lax.psum(lax.psum((weight_term, bias_term), 'rep'), 'row')]
    ppermute x16, waiting for transfers between devices: 36.6 us -> 41.3 us  [passed_along(): return lax.ppermute(value, axis, pairs)]
  transfers between devices with their start and end apart: 17 -> 18, of which waited for: 15 -> 16; matrix products, arithmetic and copies ran while one was open for 17% -> 16% of each run, Pallas kernels for 0% -> 0%
where the time goes in v1:
time: 422 us; the launch traced here: 421 us
  waiting for transfers between devices  159 us (38%)
  starting transfers between devices  84.7 us (20%)
  blocking collectives  55.8 us (13%)
  matrix products  40.3 us (10%)
  other arithmetic  36.5 us (9%)
  local copies, waits for them, and re-layouts  28.9 us (7%)
  between operations  15 us (4%)
    psum x1, waiting for transfers between devices, local(): lax.psum(lax.psum((weight_term, bias_term), 'rep'), 'row')  113 us
    ppermute x16, starting transfers between devices, passed_along(): return lax.ppermute(value, axis, pairs)  84.6 us
    psum x1, blocking collectives, local(): lax.psum(lax.psum((weight_term, bias_term), 'rep'), 'row')  42.6 us
    ppermute x16, waiting for transfers between devices, passed_along(): return lax.ppermute(value, axis, pairs)  41.3 us
    dot_general x16, matrix products, section_term(): jnp.einsum('tab,tbf->taf', tile_block, sources, preferred_element_type=jn...  22.4 us
    lt x16, other arithmetic, section_term(): usable = jnp.arange(slot_index.shape[0], dtype=jnp.int32) < counts  18.3 us
    dot_general x16, matrix products, section_term(): jnp.einsum('nt,taf->naf', placing, product, precision=lax.Precision.HIGHEST)  16.3 us
    gather x16, local copies, waits for them, and re-layouts, section_term(): sources = jnp.take(blocks, slot_index[:, 1], axis=0)  10.5 us
  transfers between devices with their start and end apart: 18, of which 16 were waited for; matrix products, arithmetic and copies ran while one was open for 16% of the time, Pallas kernels for 0%

profile of v1, /device:TPU:0, one launch (start us, length us, event | category | flops | bytes accessed | tf_op | source)
XLA Modules:
  0.0 420.6 jit_solution(7674333644690898593)
XLA Ops:
  7.2 4.1 collective-permute-start
  23.5 1.6 fusion.216
  25.8 1.2 iota_compare_fusion.30
  29.5 1.3 iota_compare_fusion.28
  38.3 1.6 fusion.215
  51.0 3.5 all_gather.3
  56.1 3.3 collective-permute-start.1
  60.0 1.4 fusion.48
  62.5 2.1 collective-permute-done.1
  65.2 1.4 fusion.46
  67.0 6.1 %collective-permute-start.2 = (bf16[512,256]{1,0:T(8,128)(2,1)S(1)}, bf16[512,256]{1,0:T(8,128)(2,1)S(1)}, u32[]{:S(2)}, u32[]{:S(2)}) collective-permute-start(bf16[512,256]{1,0:T(8,128)(2,1)S(1)} %collective-permute-done.1), channel_id=1, source_target_pairs={{0,30},{2,0},{4,2},{6,4},{8,6},{10,8},{12,10},{14,12},{16,14},{18,... | collective-permute-start | bytes 786440 | tf_op jit(solution)/shard_map/ppermute | solution.py:13
  73.1 1.3 convolution_add_fusion.13
  74.4 2.9 collective-permute-done.2
  78.1 1.4 fusion.44
  80.0 6.1 %collective-permute-start.3 = (bf16[512,256]{1,0:T(8,128)(2,1)S(1)}, bf16[512,256]{1,0:T(8,128)(2,1)S(1)}, u32[]{:S(2)}, u32[]{:S(2)}) collective-permute-start(bf16[512,256]{1,0:T(8,128)(2,1)S(1)} %copy-done.2), channel_id=1, source_target_pairs={{0,30},{2,0},{4,2},{6,4},{8,6},{10,8},{12,10},{14,12},{16,14},{18,... | collective-permute-start | bytes 786440 | tf_op jit(solution)/shard_map/ppermute | solution.py:13
  86.1 1.3 convolution_add_fusion.12
  87.4 2.6 collective-permute-done.3
  90.8 1.4 fusion.42
  92.7 6.1 %collective-permute-start.4 = (bf16[512,256]{1,0:T(8,128)(2,1)S(1)}, bf16[512,256]{1,0:T(8,128)(2,1)S(1)}, u32[]{:S(2)}, u32[]{:S(2)}) collective-permute-start(bf16[512,256]{1,0:T(8,128)(2,1)S(1)} %copy-done.4), channel_id=1, source_target_pairs={{0,30},{2,0},{4,2},{6,4},{8,6},{10,8},{12,10},{14,12},{16,14},{18,... | collective-permute-start | bytes 786440 | tf_op jit(solution)/shard_map/ppermute | solution.py:13
  98.8 1.3 convolution_add_fusion.11
  100.1 2.6 collective-permute-done.4
  103.4 1.4 fusion.40
  105.4 6.1 %collective-permute-start.5 = (bf16[512,256]{1,0:T(8,128)(2,1)S(1)}, bf16[512,256]{1,0:T(8,128)(2,1)S(1)}, u32[]{:S(2)}, u32[]{:S(2)}) collective-permute-start(bf16[512,256]{1,0:T(8,128)(2,1)S(1)} %copy-done.6), channel_id=1, source_target_pairs={{0,30},{2,0},{4,2},{6,4},{8,6},{10,8},{12,10},{14,12},{16,14},{18,... | collective-permute-start | bytes 786440 | tf_op jit(solution)/shard_map/ppermute | solution.py:13
  111.5 1.3 convolution_add_fusion.10
  112.8 2.6 collective-permute-done.5
  116.1 1.4 fusion.38
  118.0 6.1 %collective-permute-start.6 = (bf16[512,256]{1,0:T(8,128)(2,1)S(1)}, bf16[512,256]{1,0:T(8,128)(2,1)S(1)}, u32[]{:S(2)}, u32[]{:S(2)}) collective-permute-start(bf16[512,256]{1,0:T(8,128)(2,1)S(1)} %copy-done.8), channel_id=1, source_target_pairs={{0,30},{2,0},{4,2},{6,4},{8,6},{10,8},{12,10},{14,12},{16,14},{18,... | collective-permute-start | bytes 786440 | tf_op jit(solution)/shard_map/ppermute | solution.py:13
  124.2 1.3 convolution_add_fusion.9
  125.4 2.6 collective-permute-done.6
  128.8 1.4 fusion.36
  130.7 6.3 %collective-permute-start.7 = (bf16[512,256]{1,0:T(8,128)(2,1)S(1)}, bf16[512,256]{1,0:T(8,128)(2,1)S(1)}, u32[]{:S(2)}, u32[]{:S(2)}) collective-permute-start(bf16[512,256]{1,0:T(8,128)(2,1)S(1)} %copy-done.10), channel_id=1, source_target_pairs={{0,30},{2,0},{4,2},{6,4},{8,6},{10,8},{12,10},{14,12},{16,14},{18,... | collective-permute-start | bytes 786440 | tf_op jit(solution)/shard_map/ppermute | solution.py:13
  137.0 1.3 convolution_add_fusion.8
  138.3 2.6 collective-permute-done.7
  141.6 1.4 fusion.34
  144.3 4.8 %all-reduce.9 = bf16[512,256]{1,0:T(8,128)(2,1)S(1)} all-reduce(f32[512,256]{1,0:T(8,128)S(1)} %bitcast.297), channel_id=1, replica_groups=mesh['row'=16,'rep'=2] {'rep'}, use_global_device_ids=true, to_apply=%region_0.2 | all-reduce | flops 131072 | bytes 786432 | tf_op jit(solution)/shard_map/psum | solution.py:52
  153.3 6.1 %collective-permute-done.8 = bf16[512,256]{1,0:T(8,128)(2,1)S(1)} collective-permute-done((bf16[512,256]{1,0:T(8,128)(2,1)S(1)}, bf16[512,256]{1,0:T(8,128)(2,1)S(1)}, u32[]{:S(2)}, u32[]{:S(2)}) %collective-permute-start.8) | collective-permute-done | bytes 262176 | tf_op jit(solution)/shard_map/ppermute | solution.py:13
  159.5 6.0 %collective-permute-start.9 = (bf16[512,256]{1,0:T(8,128)(2,1)S(1)}, bf16[512,256]{1,0:T(8,128)(2,1)S(1)}, u32[]{:S(2)}, u32[]{:S(2)}) collective-permute-start(bf16[512,256]{1,0:T(8,128)(2,1)S(1)} %broadcast_select_fusion), channel_id=1, source_target_pairs={{0,30},{2,0},{4,2},{6,4},{8,6},{10,8},{12,10},{14,12},{16,14},{18,... | collective-permute-start | bytes 786440 | tf_op jit(solution)/shard_map/ppermute | solution.py:13
  166.2 1.4 fusion.32
  168.1 4.7 %all-reduce.6.cloned.1.call-done = f32[256,256]{1,0:T(8,128)} async-done(((f32[256,256]{1,0:T(8,128)}), f32[256,256]{1,0:T(8,128)}) %all-reduce.6.cloned.1.call-update) | async-done | bytes 262160 | tf_op jit(solution)/shard_map/psum | solution.py:96
  173.4 113.3 %all-reduce.8.cloned.1.call-done = f32[256,256]{1,0:T(8,128)} async-done(((f32[256,256]{1,0:T(8,128)}), f32[256,256]{1,0:T(8,128)}) %all-reduce.8.cloned.1.call-update) | async-done | bytes 262160 | tf_op jit(solution)/shard_map/psum | solution.py:96
  286.8 1.7 broadcast_multiply_fusion
  289.2 1.4 fusion.30
  291.0 3.3 collective-permute-start.10
  294.3 1.3 convolution_add_fusion.6
  295.6 2.6 collective-permute-done.10
  298.9 1.4 fusion.28
  300.9 6.1 %collective-permute-start.11 = (bf16[512,256]{1,0:T(8,128)(2,1)S(1)}, bf16[512,256]{1,0:T(8,128)(2,1)S(1)}, u32[]{:S(2)}, u32[]{:S(2)}) collective-permute-start(bf16[512,256]{1,0:T(8,128)(2,1)S(1)} %copy-done.12), channel_id=1, source_target_pairs={{0,30},{2,0},{4,2},{6,4},{8,6},{10,8},{12,10},{14,12},{16,14},{18,... | collective-permute-start | bytes 786440 | tf_op jit(solution)/shard_map/ppermute | solution.py:13
  307.0 1.3 convolution_add_fusion.5
  308.3 2.6 collective-permute-done.11
  311.6 1.4 fusion.26
  313.5 6.1 %collective-permute-start.12 = (bf16[512,256]{1,0:T(8,128)(2,1)S(1)}, bf16[512,256]{1,0:T(8,128)(2,1)S(1)}, u32[]{:S(2)}, u32[]{:S(2)}) collective-permute-start(bf16[512,256]{1,0:T(8,128)(2,1)S(1)} %copy-done.14), channel_id=1, source_target_pairs={{0,30},{2,0},{4,2},{6,4},{8,6},{10,8},{12,10},{14,12},{16,14},{18,... | collective-permute-start | bytes 786440 | tf_op jit(solution)/shard_map/ppermute | solution.py:13
  320.9 2.7 collective-permute-done.12
  324.3 1.4 fusion.24
  326.2 6.4 %collective-permute-start.13 = (bf16[512,256]{1,0:T(8,128)(2,1)S(1)}, bf16[512,256]{1,0:T(8,128)(2,1)S(1)}, u32[]{:S(2)}, u32[]{:S(2)}) collective-permute-start(bf16[512,256]{1,0:T(8,128)(2,1)S(1)} %copy-done.16), channel_id=1, source_target_pairs={{0,30},{2,0},{4,2},{6,4},{8,6},{10,8},{12,10},{14,12},{16,14},{18,... | collective-permute-start | bytes 786440 | tf_op jit(solution)/shard_map/ppermute | solution.py:13
  333.8 2.7 collective-permute-done.13
  337.2 1.4 fusion.22
  339.1 6.1 %collective-permute-start.14 = (bf16[512,256]{1,0:T(8,128)(2,1)S(1)}, bf16[512,256]{1,0:T(8,128)(2,1)S(1)}, u32[]{:S(2)}, u32[]{:S(2)}) collective-permute-start(bf16[512,256]{1,0:T(8,128)(2,1)S(1)} %copy-done.18), channel_id=1, source_target_pairs={{0,30},{2,0},{4,2},{6,4},{8,6},{10,8},{12,10},{14,12},{16,14},{18,... | collective-permute-start | bytes 786440 | tf_op jit(solution)/shard_map/ppermute | solution.py:13
  345.8 3.3 collective-permute-done.14
  349.8 1.4 fusion.20
  351.7 6.1 %collective-permute-start.15 = (bf16[512,256]{1,0:T(8,128)(2,1)S(1)}, bf16[512,256]{1,0:T(8,128)(2,1)S(1)}, u32[]{:S(2)}, u32[]{:S(2)}) collective-permute-start(bf16[512,256]{1,0:T(8,128)(2,1)S(1)} %copy-done.20), channel_id=1, source_target_pairs={{0,30},{2,0},{4,2},{6,4},{8,6},{10,8},{12,10},{14,12},{16,14},{18,... | collective-permute-start | bytes 786440 | tf_op jit(solution)/shard_map/ppermute | solution.py:13
  358.5 3.3 collective-permute-done.15
  362.4 1.4 fusion.18
  365.0 4.8 %all-reduce.10 = (bf16[512,256]{1,0:T(8,128)(2,1)S(1)}, f32[256]{0:T(256)S(1)}) all-reduce(f32[512,256]{1,0:T(8,128)S(1)} %bitcast.296, f32[256]{0:T(256)S(1)} %copy-done.22), channel_id=1, replica_groups=mesh['row'=16,'rep'=2] {'rep'}, use_global_device_ids=true, to_apply=%region_1.3 | all-reduce | flops 131328 | bytes 788480 | tf_op jit(solution)/shard_map/psum | solution.py:52
  370.5 42.6 %psum.47 = f32[256]{0:T(256)S(1)} all-reduce(f32[256]{0:T(256)S(1)} %get-tuple-element.6), channel_id=1, replica_groups=mesh['row'=16,'rep'=2] {'row'}, use_global_device_ids=true, to_apply=%region_6.8 | all-reduce | flops 256 | bytes 2048 | tf_op jit(solution)/shard_map/psum | solution.py:96
  (190 shorter events, 65.9 us)
Async XLA Ops:
  7.2 141.9 %copy-start = (bf16[256,256]{1,0:T(8,128)(2,1)S(1)}, bf16[256,256]{1,0:T(8,128)(2,1)}, u32[]{:S(2)}) copy-start(bf16[256,256]{1,0:T(8,128)(2,1)} %param.13) | copy-start | bytes 393220
  7.2 165.6 %all-reduce.6.cloned.1.call-start = ((), (), s32[]{:S(2)}) async-start(), calls=%async_computation | async-start | bytes 524288 | tf_op jit(solution)/shard_map/psum | solution.py:96
  7.2 47.9 %collective-permute-start = (bf16[512,256]{1,0:T(8,128)(2,1)}, bf16[512,256]{1,0:T(8,128)(2,1)S(1)}, u32[]{:S(2)}, u32[]{:S(2)}) collective-permute-start(bf16[512,256]{1,0:T(8,128)(2,1)} %param.12), channel_id=1, source_target_pairs={{0,16},{2,18},{4,20},{6,22},{8,24},{10,26},{12,28},{14,30},{16,0},... | collective-permute-start | bytes 786440 | tf_op jit(solution)/shard_map/ppermute | solution.py:13
  56.1 8.4 %collective-permute-start.1 = (bf16[512,256]{1,0:T(8,128)(2,1)S(1)}, bf16[512,256]{1,0:T(8,128)(2,1)S(1)}, u32[]{:S(2)}, u32[]{:S(2)}) collective-permute-start(bf16[512,256]{1,0:T(8,128)(2,1)S(1)} %broadcast_select_fusion.1), channel_id=1, source_target_pairs={{0,30},{2,0},{4,2},{6,4},{8,6},{10,8},{12,10},{14,12},{16,14},{18,... | collective-permute-start | bytes 786440 | tf_op jit(solution)/shard_map/ppermute | solution.py:13
  67.0 10.3 %collective-permute-start.2 = (bf16[512,256]{1,0:T(8,128)(2,1)S(1)}, bf16[512,256]{1,0:T(8,128)(2,1)S(1)}, u32[]{:S(2)}, u32[]{:S(2)}) collective-permute-start(bf16[512,256]{1,0:T(8,128)(2,1)S(1)} %collective-permute-done.1), channel_id=1, source_target_pairs={{0,30},{2,0},{4,2},{6,4},{8,6},{10,8},{12,10},{14,12},{16,14},{18,... | collective-permute-start | bytes 786440 | tf_op jit(solution)/shard_map/ppermute | solution.py:13
  77.4 0.7 copy-start.1
  78.1 1.9 copy-start.2
  80.0 10.0 %collective-permute-start.3 = (bf16[512,256]{1,0:T(8,128)(2,1)S(1)}, bf16[512,256]{1,0:T(8,128)(2,1)S(1)}, u32[]{:S(2)}, u32[]{:S(2)}) collective-permute-start(bf16[512,256]{1,0:T(8,128)(2,1)S(1)} %copy-done.2), channel_id=1, source_target_pairs={{0,30},{2,0},{4,2},{6,4},{8,6},{10,8},{12,10},{14,12},{16,14},{18,... | collective-permute-start | bytes 786440 | tf_op jit(solution)/shard_map/ppermute | solution.py:13
  90.0 0.7 copy-start.3
  90.8 1.9 copy-start.4
  92.7 10.0 %collective-permute-start.4 = (bf16[512,256]{1,0:T(8,128)(2,1)S(1)}, bf16[512,256]{1,0:T(8,128)(2,1)S(1)}, u32[]{:S(2)}, u32[]{:S(2)}) collective-permute-start(bf16[512,256]{1,0:T(8,128)(2,1)S(1)} %copy-done.4), channel_id=1, source_target_pairs={{0,30},{2,0},{4,2},{6,4},{8,6},{10,8},{12,10},{14,12},{16,14},{18,... | collective-permute-start | bytes 786440 | tf_op jit(solution)/shard_map/ppermute | solution.py:13
  102.7 0.7 copy-start.5
  103.4 1.9 copy-start.6
  105.4 10.0 %collective-permute-start.5 = (bf16[512,256]{1,0:T(8,128)(2,1)S(1)}, bf16[512,256]{1,0:T(8,128)(2,1)S(1)}, u32[]{:S(2)}, u32[]{:S(2)}) collective-permute-start(bf16[512,256]{1,0:T(8,128)(2,1)S(1)} %copy-done.6), channel_id=1, source_target_pairs={{0,30},{2,0},{4,2},{6,4},{8,6},{10,8},{12,10},{14,12},{16,14},{18,... | collective-permute-start | bytes 786440 | tf_op jit(solution)/shard_map/ppermute | solution.py:13
  115.4 0.7 copy-start.7
  116.1 1.9 copy-start.8
  118.0 10.0 %collective-permute-start.6 = (bf16[512,256]{1,0:T(8,128)(2,1)S(1)}, bf16[512,256]{1,0:T(8,128)(2,1)S(1)}, u32[]{:S(2)}, u32[]{:S(2)}) collective-permute-start(bf16[512,256]{1,0:T(8,128)(2,1)S(1)} %copy-done.8), channel_id=1, source_target_pairs={{0,30},{2,0},{4,2},{6,4},{8,6},{10,8},{12,10},{14,12},{16,14},{18,... | collective-permute-start | bytes 786440 | tf_op jit(solution)/shard_map/ppermute | solution.py:13
  128.0 0.7 copy-start.9
  128.8 1.9 copy-start.10
  130.7 10.2 %collective-permute-start.7 = (bf16[512,256]{1,0:T(8,128)(2,1)S(1)}, bf16[512,256]{1,0:T(8,128)(2,1)S(1)}, u32[]{:S(2)}, u32[]{:S(2)}) collective-permute-start(bf16[512,256]{1,0:T(8,128)(2,1)S(1)} %copy-done.10), channel_id=1, source_target_pairs={{0,30},{2,0},{4,2},{6,4},{8,6},{10,8},{12,10},{14,12},{16,14},{18,... | collective-permute-start | bytes 786440 | tf_op jit(solution)/shard_map/ppermute | solution.py:13
  141.6 1.9 copy-start.28
  141.6 1.9 copy-start.35
  143.5 5.6 %copy-start.21 = (bf16[512,256]{1,0:T(8,128)(2,1)S(1)}, bf16[512,256]{1,0:T(8,128)(2,1)}, u32[]{:S(2)}) copy-start(bf16[512,256]{1,0:T(8,128)(2,1)} %all_gather.3) | copy-start | bytes 786436
  143.5 5.6 %copy-start.37 = (f32[256]{0:T(256)S(1)}, f32[256]{0:T(256)}, u32[]{:S(2)}) copy-start(f32[256]{0:T(256)} %param.14) | copy-start | bytes 3076
  149.5 16.7 %copy-start.34 = (pred[8]{0:T(512)(128)(4,1)S(1)}, pred[8]{0:T(512)(128)(4,1)}, u32[]{:S(2)}) copy-start(pred[8]{0:T(512)(128)(4,1)} %get-tuple-element.21) | copy-start | bytes 28
  149.8 9.6 %collective-permute-start.8 = (bf16[512,256]{1,0:T(8,128)(2,1)S(1)}, bf16[512,256]{1,0:T(8,128)(2,1)S(1)}, u32[]{:S(2)}, u32[]{:S(2)}) collective-permute-start(bf16[512,256]{1,0:T(8,128)(2,1)S(1)} %convolution_convert_fusion), channel_id=1, source_target_pairs={{0,16},{2,18},{4,20},{6,22},{8,24},{10,26},{12,28},{14,30},{16,0},... | collective-permute-start | bytes 786440 | tf_op jit(solution)/shard_map/ppermute | solution.py:13
  152.0 134.8 %all-reduce.8.cloned.1.call-start = ((), (), s32[]{:S(2)}) async-start(), calls=%async_computation.1 | async-start | bytes 524288 | tf_op jit(solution)/shard_map/psum | solution.py:96
  159.5 129.0 %collective-permute-start.9 = (bf16[512,256]{1,0:T(8,128)(2,1)S(1)}, bf16[512,256]{1,0:T(8,128)(2,1)S(1)}, u32[]{:S(2)}, u32[]{:S(2)}) collective-permute-start(bf16[512,256]{1,0:T(8,128)(2,1)S(1)} %broadcast_select_fusion), channel_id=1, source_target_pairs={{0,30},{2,0},{4,2},{6,4},{8,6},{10,8},{12,10},{14,12},{16,14},{18,... | collective-permute-start | bytes 786440 | tf_op jit(solution)/shard_map/ppermute | solution.py:13
  166.2 6.6 %copy-start.23 = (s32[8]{0:T(128)S(1)}, s32[8]{0:T(128)}, u32[]{:S(2)}) copy-start(s32[8]{0:T(128)} %get-tuple-element.89) | copy-start | bytes 100
  166.2 6.6 %copy-start.29 = (pred[8]{0:T(512)(128)(4,1)S(1)}, pred[8]{0:T(512)(128)(4,1)}, u32[]{:S(2)}) copy-start(pred[8]{0:T(512)(128)(4,1)} %iota_compare_fusion.23) | copy-start | bytes 28
  168.1 121.1 %copy-start.32 = (pred[8]{0:T(512)(128)(4,1)S(1)}, pred[8]{0:T(512)(128)(4,1)}, u32[]{:S(2)}) copy-start(pred[8]{0:T(512)(128)(4,1)} %get-tuple-element.19) | copy-start | bytes 28
  291.0 7.2 %collective-permute-start.10 = (bf16[512,256]{1,0:T(8,128)(2,1)S(1)}, bf16[512,256]{1,0:T(8,128)(2,1)S(1)}, u32[]{:S(2)}, u32[]{:S(2)}) collective-permute-start(bf16[512,256]{1,0:T(8,128)(2,1)S(1)} %collective-permute-done.9), channel_id=1, source_target_pairs={{0,30},{2,0},{4,2},{6,4},{8,6},{10,8},{12,10},{14,12},{16,14},{18,... | collective-permute-start | bytes 786440 | tf_op jit(solution)/shard_map/ppermute | solution.py:13
  298.2 0.7 copy-start.11
  298.9 1.9 copy-start.12
  300.9 10.0 %collective-permute-start.11 = (bf16[512,256]{1,0:T(8,128)(2,1)S(1)}, bf16[512,256]{1,0:T(8,128)(2,1)S(1)}, u32[]{:S(2)}, u32[]{:S(2)}) collective-permute-start(bf16[512,256]{1,0:T(8,128)(2,1)S(1)} %copy-done.12), channel_id=1, source_target_pairs={{0,30},{2,0},{4,2},{6,4},{8,6},{10,8},{12,10},{14,12},{16,14},{18,... | collective-permute-start | bytes 786440 | tf_op jit(solution)/shard_map/ppermute | solution.py:13
  310.9 0.7 copy-start.13
  311.6 1.9 copy-start.14
  313.5 10.0 %collective-permute-start.12 = (bf16[512,256]{1,0:T(8,128)(2,1)S(1)}, bf16[512,256]{1,0:T(8,128)(2,1)S(1)}, u32[]{:S(2)}, u32[]{:S(2)}) collective-permute-start(bf16[512,256]{1,0:T(8,128)(2,1)S(1)} %copy-done.14), channel_id=1, source_target_pairs={{0,30},{2,0},{4,2},{6,4},{8,6},{10,8},{12,10},{14,12},{16,14},{18,... | collective-permute-start | bytes 786440 | tf_op jit(solution)/shard_map/ppermute | solution.py:13
  323.6 0.7 copy-start.15
  324.3 8.3 %copy-start.25 = (s32[8]{0:T(128)S(1)}, s32[8]{0:T(128)}, u32[]{:S(2)}) copy-start(s32[8]{0:T(128)} %get-tuple-element.85) | copy-start | bytes 100
  324.3 1.9 copy-start.16
  326.2 10.2 %collective-permute-start.13 = (bf16[512,256]{1,0:T(8,128)(2,1)S(1)}, bf16[512,256]{1,0:T(8,128)(2,1)S(1)}, u32[]{:S(2)}, u32[]{:S(2)}) collective-permute-start(bf16[512,256]{1,0:T(8,128)(2,1)S(1)} %copy-done.16), channel_id=1, source_target_pairs={{0,30},{2,0},{4,2},{6,4},{8,6},{10,8},{12,10},{14,12},{16,14},{18,... | collective-permute-start | bytes 786440 | tf_op jit(solution)/shard_map/ppermute | solution.py:13
  336.4 0.7 copy-start.17
  337.1 8.1 %copy-start.24 = (s32[8]{0:T(128)S(1)}, s32[8]{0:T(128)}, u32[]{:S(2)}) copy-start(s32[8]{0:T(128)} %get-tuple-element.84) | copy-start | bytes 100
  337.1 8.1 %copy-start.33 = (pred[8]{0:T(512)(128)(4,1)S(1)}, pred[8]{0:T(512)(128)(4,1)}, u32[]{:S(2)}) copy-start(pred[8]{0:T(512)(128)(4,1)} %iota_compare_fusion.18) | copy-start | bytes 28
  337.2 1.9 copy-start.18
  339.1 10.0 %collective-permute-start.14 = (bf16[512,256]{1,0:T(8,128)(2,1)S(1)}, bf16[512,256]{1,0:T(8,128)(2,1)S(1)}, u32[]{:S(2)}, u32[]{:S(2)}) collective-permute-start(bf16[512,256]{1,0:T(8,128)(2,1)S(1)} %copy-done.18), channel_id=1, source_target_pairs={{0,30},{2,0},{4,2},{6,4},{8,6},{10,8},{12,10},{14,12},{16,14},{18,... | collective-permute-start | bytes 786440 | tf_op jit(solution)/shard_map/ppermute | solution.py:13
  349.1 0.7 copy-start.19
  349.8 8.1 %copy-start.27 = (s32[8]{0:T(128)S(1)}, s32[8]{0:T(128)}, u32[]{:S(2)}) copy-start(s32[8]{0:T(128)} %get-tuple-element.83) | copy-start | bytes 100
  349.8 8.1 %copy-start.31 = (pred[8]{0:T(512)(128)(4,1)S(1)}, pred[8]{0:T(512)(128)(4,1)}, u32[]{:S(2)}) copy-start(pred[8]{0:T(512)(128)(4,1)} %iota_compare_fusion.17) | copy-start | bytes 28
  349.8 1.9 copy-start.20
  351.7 10.6 %copy-start.30 = (pred[8]{0:T(512)(128)(4,1)S(1)}, pred[8]{0:T(512)(128)(4,1)}, u32[]{:S(2)}) copy-start(pred[8]{0:T(512)(128)(4,1)} %get-tuple-element.7) | copy-start | bytes 28
  351.7 10.0 %collective-permute-start.15 = (bf16[512,256]{1,0:T(8,128)(2,1)S(1)}, bf16[512,256]{1,0:T(8,128)(2,1)S(1)}, u32[]{:S(2)}, u32[]{:S(2)}) collective-permute-start(bf16[512,256]{1,0:T(8,128)(2,1)S(1)} %copy-done.20), channel_id=1, source_target_pairs={{0,30},{2,0},{4,2},{6,4},{8,6},{10,8},{12,10},{14,12},{16,14},{18,... | collective-permute-start | bytes 786440 | tf_op jit(solution)/shard_map/ppermute | solution.py:13
  362.3 1.9 copy-start.26
  362.4 1.9 copy-start.36
  364.2 0.8 copy-start.22
Sparse Core Ops, SparseCore 0:
  152.1 20.6 all-reduce.5
  178.8 107.8 all-reduce.7
